TPU v7x, 32 devices: a whole 2x2x4 slice. The times are simulated.
32 devices in a mesh: blk: 8 (over z, y), gy: 4 (over x, core).
Axes of the slice: x: 2, y: 2, z: 4, core: 2. Of those that a mesh axis runs over, the one named last changes fastest.
Arguments:
- image: float32 [1, 2048, 2048], P(None, 'blk', 'gy'), may hold values from -6 to 6
- measured: float32 [1, 16, 2816], P(None, 'blk'), may hold values from -6 to 6
- row_weight: float32 [16, 2816], P('blk'), may hold values from 0.25 to 2
- col_weight: float32 [2048, 2048], P('blk', 'gy'), may hold values from 1 to 8
- band_weight: bfloat16 [16, 2048, 128], P('blk', 'gy'), may hold values from -0.01171875 to 0.01171875
- band_shift: int32 [16, 8], replicated, may hold values from 0 to 3
Outputs:
- updated: float32 [1, 2048, 2048], P(None, 'blk', 'gy')
Inputs may be any that keep to these rules, and one draw needn't show every extreme that they name: band_shift[t, s] is the number of panels by which slab s's footprint under tilt t starts beyond panel s * 2.
All inputs are finite; a program needn't handle non-finite values.
Results may differ from a plain program's by a relative error of at most 0.0025.
Values may be sent and summed in bfloat16 or wider, within the bound.
A program may use at most 64 MiB of HBM per device.

v0:
```python
import math
import jax
import jax.numpy as jnp
from jax import lax
from jax.sharding import PartitionSpec as P

PW = 128
SMOOTH = 0.25


def with_halo(cells, sides, width):
    for axis, dim in sides:
        count = lax.axis_size(axis)
        ends = count - 1
        head = lax.slice_in_dim(cells, 0, width, axis=dim)
        tail = lax.slice_in_dim(cells, cells.shape[dim] - width, cells.shape[dim], axis=dim)
        cells = jnp.concatenate(
            [
                lax.ppermute(tail, axis, [(i, (i + 1) % count) for i in range(ends)]),
                cells,
                lax.ppermute(head, axis, [((i + 1) % count, i) for i in range(ends)]),
            ],
            axis=dim,
        )
    return cells


def shift_rows(rows, direction):
    col_count = rows.shape[-2]
    bit_count = (col_count - 1).bit_length()
    column_index = jnp.arange(col_count, dtype=jnp.int32)[:, None]
    for level in range(bit_count):
        moved = jnp.roll(rows, direction * (1 << level), axis=-1)
        chosen = column_index >> level & 1 == 1
        rows = jnp.where(chosen, moved, rows)
    return rows


def diagonal_sum(product):
    leading = product.shape[:-2]
    col_count, band_width = product.shape[-2:]
    keep_pads = [(0, 0)] * (len(leading) + 1)
    padded = jnp.pad(product, keep_pads + [(0, col_count)])
    return jnp.sum(shift_rows(padded, 1), axis=-2)


def band_rows(panels, col_count, band_width):
    leading = panels.shape[:-1]
    window_len = panels.shape[-1]
    repeated = jnp.broadcast_to(panels[..., None, :], leading + (col_count, window_len))
    return shift_rows(repeated, -1)[..., :band_width]


def per_device(image, measured, row_weight, col_weight, band_weight, band_shift):
    row_count, col_count, depth_count = image.shape
    local_tilts = measured.shape[1]
    detector_len = measured.shape[2]
    band_width = band_weight.shape[2]
    window_len = col_count + band_width
    block_count = lax.axis_size("blk")
    myself = lax.axis_index("blk")
    tilt_count = local_tilts * block_count
    per_slab = col_count // PW
    zero_index = jnp.int32(0)
    copies = image.astype(jnp.bfloat16)
    slab_bins = ((jnp.arange(block_count, dtype=jnp.int32) * per_slab)[None, :] + band_shift) * PW
    first_tilt = myself * local_tilts
    own_bins = lax.dynamic_slice_in_dim(slab_bins, first_tilt, local_tilts, 0)
    group_size = math.gcd(tilt_count, 8)
    all_weights = lax.all_gather(band_weight, "blk", axis=0, tiled=True)
    weight_groups = all_weights.reshape(
        tilt_count // group_size, group_size, depth_count, band_width
    )

    def place_windows(running, windows, source):
        for tilt_slot in range(local_tilts):
            offset = own_bins[tilt_slot, source]
            corner = (zero_index, jnp.int32(tilt_slot), offset)
            current = lax.dynamic_slice(running, corner, (row_count, 1, window_len))
            running = lax.dynamic_update_slice(
                running, current + windows[tilt_slot][:, None, :], corner
            )
        return running

    initial = jnp.zeros((row_count, local_tilts, detector_len), jnp.float32)

    def project_group(weights):
        product = jnp.einsum("yiz,tzd->tyid", copies, weights, preferred_element_type=jnp.float32)
        return diagonal_sum(product)

    windows = lax.map(project_group, weight_groups)
    windows = windows.reshape(block_count, local_tilts, row_count, window_len)
    received = lax.all_to_all(windows, "blk", split_axis=0, concat_axis=0, tiled=True)

    def add_source(source, running):
        return place_windows(
            running, lax.dynamic_index_in_dim(received, source, 0, keepdims=False), source
        )

    partial_sum = lax.fori_loop(0, block_count, add_source, initial)
    projection = lax.psum(partial_sum, "gy")
    weighted = (row_weight[None] * (measured - projection)).astype(jnp.bfloat16)

    def cut_panels(slab_offsets):
        pieces = [
            lax.dynamic_slice(
                weighted[:, tilt_slot],
                (zero_index, slab_offsets[tilt_slot]),
                (row_count, window_len),
            )
            for tilt_slot in range(local_tilts)
        ]
        return jnp.stack(pieces, axis=1)

    outgoing = jax.vmap(cut_panels, in_axes=1, out_axes=1)(own_bins)
    arrived = lax.all_to_all(outgoing, "blk", split_axis=1, concat_axis=1, tiled=True)
    panels = arrived.reshape(row_count, tilt_count, window_len)
    panel_groups = panels.reshape(
        row_count, tilt_count // group_size, group_size, window_len
    ).transpose(1, 0, 2, 3)

    def back_group(running, operands):
        panel_part, weight_part = operands
        sheared = band_rows(panel_part, col_count, band_width)
        added = jnp.einsum(
            "ytid,tzd->yiz", sheared, weight_part, preferred_element_type=jnp.float32
        )
        return (running + added, None)

    start_back = jnp.zeros((row_count, col_count, depth_count), jnp.float32)
    backed, leftover = lax.scan(back_group, start_back, (panel_groups, weight_groups))
    padded_depth = with_halo(image.astype(jnp.bfloat16), (("gy", 2),), 1).astype(image.dtype)
    return (
        image
        + col_weight[None] * backed
        + SMOOTH * (padded_depth[:, :, :-2] + padded_depth[:, :, 2:] - 2.0 * image)
    )


def solution(mesh):
    return jax.shard_map(
        per_device,
        mesh=mesh,
        in_specs=(
            P(None, "blk", "gy"),
            P(None, "blk", None),
            P("blk", None),
            P("blk", "gy"),
            P("blk", "gy", None),
            P(),
        ),
        out_specs=P(None, "blk", "gy"),
        check_vma=False,
    )
```

profile of v0, /device:TPU:0, one launch (start us, length us, event | category | flops | bytes accessed | tf_op | source)
XLA Modules:
  0.0 203.8 jit_solution(14922307778124006677)
XLA Ops:
  6.5 0.7 all-gather.2.cloned.1.call-update
  7.3 1.1 convert_element_type.22
  8.3 0.7 fusion.22
  9.0 3.0 %collective-permute-start = (bf16[1,256,1]{2,1,0:T(8,128)(2,1)}, bf16[1,256,1]{2,1,0:T(8,128)(2,1)}, u32[]{:S(2)}, u32[]{:S(2)}) collective-permute-start(bf16[1,256,1]{2,1,0:T(8,128)(2,1)} %get-tuple-element.283), channel_id=1, source_target_pairs={{0,1},{1,2},{2,3},{4,5},{5,6},{6,7},{8,9},{9,10},{10,11},{12,13},{... | collective-permute-start | bytes 1544 | tf_op jit(solution)/shard_map/ppermute | solution.py:19
  12.0 1.3 collective-permute-start.1
  13.3 0.8 add_multiply_fusion
  14.8 0.7 slice_reduce_fusion.1
  15.5 46.0 %all-gather.2.cloned.1.call-done = bf16[16,512,128]{2,1,0:T(8,128)(2,1)} async-done(((bf16[2,512,128]{2,1,0:T(8,128)(2,1)}), bf16[16,512,128]{2,1,0:T(8,128)(2,1)}) %all-gather.2.cloned.1.call-update) | async-done | bytes 2097168 | tf_op jit(solution)/shard_map/all_gather | solution.py:70
  61.5 14.9 %while.38 = (s32[]{:T(128)}, f32[2,8,1,384]{3,2,1,0:T(1,128)}, bf16[2,8,512,128]{3,2,1,0:T(8,128)(2,1)}, bf16[1,256,512]{2,1,0:T(8,128)(2,1)S(1)}, s32[]{:T(128)}) while((s32[]{:T(128)}, f32[2,8,1,384]{3,2,1,0:T(1,128)}, bf16[2,8,512,128]{3,2,1,0:T(8,128)(2,1)}, bf16[1,256,512]{2,1,0:T(8,128)(2,1)S(1)}, s32[]{:T(128)}) %tuple.126), condition=%wide.region_2.3_spmd, body=%wide.region_0.2_spmd.sunk | while | flops 281021440 | bytes 108389440 | solution.py:91
  61.5 1.7 convolution_bitcast_fusion.3
  69.0 1.7 convolution_bitcast_fusion.3
  76.4 3.3 %all-to-all-start = ((f32[8,2,1,384]{3,2,1,0:T(1,128)}), f32[8,2,1,384]{3,2,1,0:T(1,128)S(1)}, u32[]{:S(2)}, u32[]{:S(2)}) async-start(f32[8,2,1,384]{3,2,1,0:T(1,128)} %bitcast.12), calls=%async_computation | async-start | bytes 49152 | tf_op jit(solution)/shard_map/all_to_all | solution.py:93
  79.9 6.4 %all-to-all-done = f32[8,2,1,384]{3,2,1,0:T(1,128)S(1)} async-done(((f32[8,2,1,384]{3,2,1,0:T(1,128)}), f32[8,2,1,384]{3,2,1,0:T(1,128)S(1)}, u32[]{:S(2)}, u32[]{:S(2)}) %all-to-all-start) | async-done | bytes 24608 | tf_op jit(solution)/shard_map/all_to_all | solution.py:93
  86.3 35.3 %while.39 = (s32[]{:T(128)}, f32[1,2,2816]{2,1,0:T(2,128)S(1)}, s32[2,8]{1,0:T(2,128)S(1)}, f32[8,2,1,384]{3,2,1,0:T(1,128)S(1)}, s32[]{:T(128)}, /*index=5*/s32[]{:T(128)}, s32[]{:T(128)}, s32[]{}) while((s32[]{:T(128)}, f32[1,2,2816]{2,1,0:T(2,128)S(1)}, s32[2,8]{1,0:T(2,128)S(1)}, f32[8,2,1,384]{3,2,1,0:T(1,128)S(1)}, s32[]{:T(128)}, ...), condition=%wide.region_4.5_spmd, body=%wide.region_3.4_spmd.sunk | while | flops 777 | bytes 15573 | solution.py:100
  121.7 10.3 %psum.7 = f32[1,2,2816]{2,1,0:T(2,128)S(1)} all-reduce(f32[1,2,2816]{2,1,0:T(2,128)S(1)} %get-tuple-element.160), channel_id=1, replica_groups=mesh['blk'=8,'gy'=4] {'gy'}, use_global_device_ids=true, to_apply=%region_5.6 | all-reduce | flops 5632 | bytes 45056 | tf_op jit(solution)/shard_map/psum | solution.py:101
  132.0 11.8 %while.40 = (s32[]{:T(128)}, bf16[1,2816]{1,0:T(2,128)(2,1)S(1)}, s32[8,2]{0,1:T(2,128)S(1)}, bf16[8,1,384]{2,0,1:T(8,128)(2,1)S(1)}, s32[]{:T(128)}, /*index=5*/s32[]{:T(128)}) while((s32[]{:T(128)}, bf16[1,2816]{1,0:T(2,128)(2,1)S(1)}, s32[8,2]{0,1:T(2,128)S(1)}, bf16[8,1,384]{2,0,1:T(8,128)(2,1)S(1)}, s32[]{:T(128)}, /*index=5*/s32[]{:T(128)}) %tuple.118), condition=%wide.while_cond, body=%wide.while_body.sunk | while | flops 2 | bytes 3177 | solution.py:106
  132.7 0.8 dynamic-slice_bitcast_fusion.6
  134.2 0.8 dynamic-slice_bitcast_fusion.6
  135.7 0.8 dynamic-slice_bitcast_fusion.6
  137.2 0.8 dynamic-slice_bitcast_fusion.6
  138.6 0.8 dynamic-slice_bitcast_fusion.6
  140.1 0.8 dynamic-slice_bitcast_fusion.6
  141.6 0.8 dynamic-slice_bitcast_fusion.6
  143.1 0.8 dynamic-slice_bitcast_fusion.6
  143.9 10.7 %while.41 = (s32[]{:T(128)}, bf16[1,2816]{1,0:T(2,128)(2,1)S(1)}, s32[8,2]{0,1:T(2,128)S(1)}, bf16[8,1,384]{2,0,1:T(8,128)(2,1)S(1)}, s32[]{:T(128)}, /*index=5*/s32[]{:T(128)}) while((s32[]{:T(128)}, bf16[1,2816]{1,0:T(2,128)(2,1)S(1)}, s32[8,2]{0,1:T(2,128)S(1)}, bf16[8,1,384]{2,0,1:T(8,128)(2,1)S(1)}, s32[]{:T(128)}, /*index=5*/s32[]{:T(128)}) %tuple.115), condition=%wide.while_cond.1, body=%wide.while_body.1.sunk | while | flops 2 | bytes 3177 | solution.py:106
  145.8 0.7 dynamic-slice_bitcast_fusion.7
  147.2 0.7 dynamic-slice_bitcast_fusion.7
  148.5 0.7 dynamic-slice_bitcast_fusion.7
  149.8 0.7 dynamic-slice_bitcast_fusion.7
  151.2 0.7 dynamic-slice_bitcast_fusion.7
  152.5 0.7 dynamic-slice_bitcast_fusion.7
  155.2 3.5 %all-to-all-start.1 = ((bf16[1,8,2,384]{3,2,0,1:T(2,128)(2,1)}), bf16[1,8,2,384]{3,2,0,1:T(2,128)(2,1)S(1)}, u32[]{:S(2)}, u32[]{:S(2)}) async-start(bf16[1,8,2,384]{3,2,0,1:T(2,128)(2,1)} %copy.33), calls=%async_computation.1 | async-start | bytes 24576 | tf_op jit(solution)/shard_map/all_to_all | solution.py:116
  158.7 1.9 maximum_convert_fusion
  160.6 4.4 %all-to-all-done.1 = bf16[1,8,2,384]{3,2,0,1:T(2,128)(2,1)S(1)} async-done(((bf16[1,8,2,384]{3,2,0,1:T(2,128)(2,1)}), bf16[1,8,2,384]{3,2,0,1:T(2,128)(2,1)S(1)}, u32[]{:S(2)}, u32[]{:S(2)}) %all-to-all-start.1) | async-done | bytes 12320 | tf_op jit(solution)/shard_map/all_to_all | solution.py:116
  165.0 29.1 %while.42 = (s32[]{:T(128)}, f32[1,256,512]{2,1,0:T(8,128)}, bf16[2,1,8,384]{3,2,0,1:T(8,128)(2,1)S(1)}, bf16[2,8,512,128]{3,2,1,0:T(8,128)(2,1)}, s32[]{:T(128)}, /*index=5*/s32[]{:T(128)}) while((s32[]{:T(128)}, f32[1,256,512]{2,1,0:T(8,128)}, bf16[2,1,8,384]{3,2,0,1:T(8,128)(2,1)S(1)}, bf16[2,8,512,128]{3,2,1,0:T(8,128)(2,1)}, ...), condition=%wide.region_7.8_spmd.clone, body=%wide.region_6.7_spmd.clone.sunk | while | flops 301471744 | bytes 67193432 | solution.py:131
  166.3 0.7 slice.372
  167.1 1.1 maximum_select_fusion.34
  168.2 0.7 slice.374
  169.1 0.7 maximum_select_fusion.35
  169.8 0.7 slice.376
  170.7 0.7 maximum_select_fusion.36
  171.4 0.7 slice.378
  172.3 0.7 maximum_select_fusion.37
  173.0 0.7 slice.380
  173.9 0.7 maximum_select_fusion.38
  174.6 0.7 slice.382
  175.5 0.7 maximum_select_fusion.39
  176.3 0.9 slice.383
  177.2 2.3 %fusion.41 = f32[1,256,512]{2,1,0:T(8,128)} fusion(bf16[2,8,512,128]{3,2,1,0:T(8,128)(2,1)S(1)} %copy-done, s32[]{:T(128)} %get-tuple-element.503, bf16[1,8,256,128]{3,2,1,0:T(8,128)(2,1)} %slice.383, bf16[1,8,256,256]{3,2,1,0:T(8,128)(2,1)S(1)} %slice.384, f32[1,256,512]{2,1,0:T(8,128)} %get-tuple-element.504, ...), kind=kOutput, calls=%fused_computation.42.clone.1 | convolution fusion | flops 270008320 | bytes 3670533 | tf_op jit(solution)/shard_map/while/body/eval_jaxpr/ytid,tzd->yiz/dot_general | solution.py:125
  180.7 0.7 slice.372
  181.6 1.1 maximum_select_fusion.34
  182.7 0.7 slice.374
  183.6 0.7 maximum_select_fusion.35
  184.3 0.7 slice.376
  185.2 0.7 maximum_select_fusion.36
  185.9 0.7 slice.378
  186.8 0.7 maximum_select_fusion.37
  187.5 0.7 slice.380
  188.4 0.7 maximum_select_fusion.38
  189.1 0.7 slice.382
  190.0 0.7 maximum_select_fusion.39
  190.8 0.9 slice.383
  191.7 2.5 %fusion.41 = f32[1,256,512]{2,1,0:T(8,128)} fusion(bf16[2,8,512,128]{3,2,1,0:T(8,128)(2,1)S(1)} %copy-done, s32[]{:T(128)} %get-tuple-element.503, bf16[1,8,256,128]{3,2,1,0:T(8,128)(2,1)} %slice.383, bf16[1,8,256,256]{3,2,1,0:T(8,128)(2,1)S(1)} %slice.384, f32[1,256,512]{2,1,0:T(8,128)} %get-tuple-element.504, ...), kind=kOutput, calls=%fused_computation.42.clone.1 | convolution fusion | flops 270008320 | bytes 3670533 | tf_op jit(solution)/shard_map/while/body/eval_jaxpr/ytid,tzd->yiz/dot_general | solution.py:125
  194.2 2.8 %fusion.19 = f32[1,256,512]{2,1,0:T(8,128)} fusion(f32[1,256,514]{2,1,0:T(8,128)} %maximum_convert_fusion, f32[1,256,512]{2,1,0:T(8,128)} %param.12, f32[1,256,512]{2,1,0:T(8,128)} %get-tuple-element.161, f32[256,512]{1,0:T(8,128)} %param.15), kind=kLoop, calls=%fused_computation.65 | loop fusion | flops 917504 | bytes 3145728 | tf_op jit(solution)/shard_map/add | solution.py:134
  (231 shorter events, 36.3 us)
Async XLA Ops:
  6.5 55.0 %all-gather.2.cloned.1.call-start = ((), (), s32[]{:S(2)}) async-start(), calls=%async_computation.2 | async-start | bytes 2359296 | tf_op jit(solution)/shard_map/all_gather | solution.py:70
  9.0 149.7 %collective-permute-start = (bf16[1,256,1]{2,1,0:T(8,128)(2,1)}, bf16[1,256,1]{2,1,0:T(8,128)(2,1)}, u32[]{:S(2)}, u32[]{:S(2)}) collective-permute-start(bf16[1,256,1]{2,1,0:T(8,128)(2,1)} %get-tuple-element.283), channel_id=1, source_target_pairs={{0,1},{1,2},{2,3},{4,5},{5,6},{6,7},{8,9},{9,10},{10,11},{12,13},{... | collective-permute-start | bytes 1544 | tf_op jit(solution)/shard_map/ppermute | solution.py:19
  12.0 146.7 %collective-permute-start.1 = (bf16[1,256,1]{2,1,0:T(8,128)(2,1)}, bf16[1,256,1]{2,1,0:T(8,128)(2,1)}, u32[]{:S(2)}, u32[]{:S(2)}) collective-permute-start(bf16[1,256,1]{2,1,0:T(8,128)(2,1)} %get-tuple-element.284), channel_id=1, source_target_pairs={{1,0},{2,1},{3,2},{5,4},{6,5},{7,6},{9,8},{10,9},{11,10},{13,12},{... | collective-permute-start | bytes 1544 | tf_op jit(solution)/shard_map/ppermute | solution.py:21
  14.2 0.6 copy-start.1
  61.5 18.3 %copy-start.5 = (s32[8]{0:T(128)S(1)}, s32[8]{0:T(128)}, u32[]{:S(2)}) copy-start(s32[8]{0:T(128)} %get-tuple-element.237) | copy-start | bytes 100
  61.5 18.3 %copy-start.6 = (s32[8]{0:T(128)S(1)}, s32[8]{0:T(128)}, u32[]{:S(2)}) copy-start(s32[8]{0:T(128)} %get-tuple-element.238) | copy-start | bytes 100
  61.5 18.3 %copy-start.2 = (s32[2,8]{0,1:T(8,128)S(1)}, s32[2,8]{0,1:T(8,128)}, u32[]{:S(2)}) copy-start(s32[2,8]{0,1:T(8,128)} %copy-done.1) | copy-start | bytes 196
  61.5 70.4 %copy-start.3 = (f32[2,2816]{1,0:T(2,128)S(1)}, f32[2,2816]{1,0:T(2,128)}, u32[]{:S(2)}) copy-start(f32[2,2816]{1,0:T(2,128)} %param.14) | copy-start | bytes 67588
  61.5 70.4 %copy-start.4 = (f32[1,2,2816]{2,1,0:T(2,128)S(1)}, f32[1,2,2816]{2,1,0:T(2,128)}, u32[]{:S(2)}) copy-start(f32[1,2,2816]{2,1,0:T(2,128)} %param.13) | copy-start | bytes 67588
  76.4 9.9 %all-to-all-start = ((f32[8,2,1,384]{3,2,1,0:T(1,128)}), f32[8,2,1,384]{3,2,1,0:T(1,128)S(1)}, u32[]{:S(2)}, u32[]{:S(2)}) async-start(f32[8,2,1,384]{3,2,1,0:T(1,128)} %bitcast.12), calls=%async_computation | async-start | bytes 49152 | tf_op jit(solution)/shard_map/all_to_all | solution.py:93
  155.2 9.8 %all-to-all-start.1 = ((bf16[1,8,2,384]{3,2,0,1:T(2,128)(2,1)}), bf16[1,8,2,384]{3,2,0,1:T(2,128)(2,1)S(1)}, u32[]{:S(2)}, u32[]{:S(2)}) async-start(bf16[1,8,2,384]{3,2,0,1:T(2,128)(2,1)} %copy.33), calls=%async_computation.1 | async-start | bytes 24576 | tf_op jit(solution)/shard_map/all_to_all | solution.py:116
  175.5 1.7 copy-start
  190.0 1.7 copy-start
Sparse Core Ops, SparseCore 0:
  9.5 51.9 all-gather.1
where the time goes:
time: 205 us; the launch traced here: 204 us
  waiting for transfers between devices  57.6 us (28%)
  local copies, waits for them, and re-layouts  49.3 us (24%)
  loops' own time  28.2 us (14%)
  other arithmetic  25.6 us (12%)
  between operations  13.6 us (7%)
  starting transfers between devices  11.1 us (5%)
  blocking collectives  10.3 us (5%)
  matrix products  8.25 us (4%)
    all_gather x1, waiting for transfers between devices, per_device(): all_weights = lax.all_gather(band_weight, 'blk', axis=0, tiled=True)  46 us
    another operation x1, loops' own time, per_device(): partial_sum = lax.fori_loop(0, block_count, add_source, initial)  27.2 us
    gather x64, local copies, waits for them, and re-layouts  22.3 us
    select_n x28, other arithmetic, shift_rows(): rows = jnp.where(chosen, moved, rows)  16.4 us
    slice x60, local copies, waits for them, and re-layouts, shift_rows(): moved = jnp.roll(rows, direction * (1 << level), axis=-1)  15.1 us
    psum x1, blocking collectives, per_device(): projection = lax.psum(partial_sum, 'gy')  10.3 us
    all_to_all x1, waiting for transfers between devices, per_device(): lax.all_to_all(windows, 'blk', split_axis=0, concat_axis=0, tiled=True)  6.42 us
    dot_general x2, matrix products, back_group(): jnp.einsum('ytid,tzd->yiz', sheared, weight_part, preferred_element_type=...  4.81 us
  transfers between devices with their start and end apart: 5, of which 3 were waited for; matrix products, arithmetic and copies ran while one was open for 25% of the time, Pallas kernels for 0%

commit v1 on v0

--- a/solution.py
+++ b/solution.py
@@ -3,9 +3,26 @@
 import jax.numpy as jnp
 from jax import lax
 from jax.sharding import PartitionSpec as P
+from jax.lax import axis_index, axis_size, ppermute
 
 PW = 128
 SMOOTH = 0.25
+
+
+def pass_blocks(work_x, k_dim, x_in):
+    state_now, back = (work_x.shape[:k_dim], work_x.shape[k_dim + 1 :])
+    lower = work_x.reshape(*state_now, x_in, -1, *back)
+    everything = jnp.moveaxis(lower, k_dim, 0)
+    return everything
+
+
+def put_weights(array_here, out_dim):
+    array_here = jnp.moveaxis(array_here, 0, out_dim)
+    d_next = array_here.shape
+    top = array_here.reshape(
+        *d_next[:out_dim], d_next[out_dim] * d_next[out_dim + 1], *d_next[out_dim + 2 :]
+    )
+    return top
 
 
 def with_halo(cells, sides, width):
@@ -90,7 +107,17 @@
 
     windows = lax.map(project_group, weight_groups)
     windows = windows.reshape(block_count, local_tilts, row_count, window_len)
-    received = lax.all_to_all(windows, "blk", split_axis=0, concat_axis=0, tiled=True)
+    local_next = axis_size("blk")
+    answer = axis_index("blk")
+    a_next, even = (local_next, answer)
+    frame_out = pass_blocks(windows, 0, a_next)
+    arrivals = [frame_out[even]]
+    for j in tuple(range(1, a_next)):
+        b_now = frame_out[even ^ j]
+        arrivals.append(ppermute(b_now, axis_name="blk", perm=[(t, t ^ j) for t in range(a_next)]))
+    fresh = jnp.stack(arrivals)
+    frame_out = fresh[even ^ jnp.arange(a_next)]
+    received = put_weights(frame_out, 0)
 
     def add_source(source, running):
         return place_windows(

time: 205 us -> 213 us (1.039)
  starting transfers between devices: 11.1 us -> 19.3 us
  loops' own time: 28.2 us -> 31.7 us
  waiting for transfers between devices: 57.6 us -> 54.8 us
    ppermute x0 -> x7, starting transfers between devices: none -> 11.4 us  [per_device(): ppermute(b_now, axis_name='blk', perm=[(t, t ^ j) for t in range(a_next)])]
    all_to_all x1 -> x0, waiting for transfers between devices: 6.42 us -> none  [per_device(): lax.all_to_all(windows, 'blk', split_axis=0, concat_axis=0, tiled=True)]
    ppermute x0 -> x7, waiting for transfers between devices: none -> 3.93 us  [per_device(): ppermute(b_now, axis_name='blk', perm=[(t, t ^ j) for t in range(a_next)])]
    another operation x1, loops' own time: 27.2 us -> 30.6 us  [per_device(): partial_sum = lax.fori_loop(0, block_count, add_source, initial)]
    all_to_all x1 -> x0, starting transfers between devices: 3.34 us -> none  [per_device(): lax.all_to_all(windows, 'blk', split_axis=0, concat_axis=0, tiled=True)]
    gather x64 -> x65, local copies, waits for them, and re-layouts: 22.3 us -> 21.5 us
  transfers between devices with their start and end apart: 5 -> 11, of which waited for: 3 -> 4; matrix products, arithmetic and copies ran while one was open for 25% -> 24% of each run, Pallas kernels for 0% -> 0%
where the time goes in v1:
time: 213 us; the launch traced here: 212 us
  waiting for transfers between devices  54.8 us (26%)
  local copies, waits for them, and re-layouts  47.3 us (22%)
  loops' own time  31.7 us (15%)
  other arithmetic  26.7 us (13%)
  starting transfers between devices  19.3 us (9%)
  between operations  13.7 us (6%)
  blocking collectives  10.3 us (5%)
  matrix products  8.24 us (4%)
    all_gather x1, waiting for transfers between devices, per_device(): all_weights = lax.all_gather(band_weight, 'blk', axis=0, tiled=True)  45.5 us
    another operation x1, loops' own time, per_device(): partial_sum = lax.fori_loop(0, block_count, add_source, initial)  30.6 us
    gather x64, local copies, waits for them, and re-layouts  20.9 us
    select_n x28, other arithmetic, shift_rows(): rows = jnp.where(chosen, moved, rows)  16.4 us
    slice x60, local copies, waits for them, and re-layouts, shift_rows(): moved = jnp.roll(rows, direction * (1 << level), axis=-1)  15.1 us
    ppermute x7, starting transfers between devices, per_device(): ppermute(b_now, axis_name='blk', perm=[(t, t ^ j) for t in range(a_next)])  11.4 us
    psum x1, blocking collectives, per_device(): projection = lax.psum(partial_sum, 'gy')  10.3 us
    dynamic_slice x8, local copies, waits for them, and re-layouts, place_windows(): offset = own_bins[tilt_slot, source]  5.15 us
  transfers between devices with their start and end apart: 11, of which 4 were waited for; matrix products, arithmetic and copies ran while one was open for 24% of the time, Pallas kernels for 0%

profile of v1, /device:TPU:0, one launch (start us, length us, event | category | flops | bytes accessed | tf_op | source)
XLA Modules:
  0.0 211.9 jit_solution(9157304032204798938)
XLA Ops:
  6.5 0.7 all-gather.2.cloned.1.call-update
  7.3 1.1 convert_element_type.22
  8.3 0.7 fusion.23
  9.0 3.0 %collective-permute-start.7 = (bf16[1,256,1]{2,1,0:T(8,128)(2,1)}, bf16[1,256,1]{2,1,0:T(8,128)(2,1)}, u32[]{:S(2)}, u32[]{:S(2)}) collective-permute-start(bf16[1,256,1]{2,1,0:T(8,128)(2,1)} %get-tuple-element.283), channel_id=1, source_target_pairs={{0,1},{1,2},{2,3},{4,5},{5,6},{6,7},{8,9},{9,10},{10,11},{12,13},{... | collective-permute-start | bytes 1544 | tf_op jit(solution)/shard_map/ppermute | solution.py:36
  12.0 1.3 collective-permute-start.8
  13.9 0.8 add_multiply_fusion
  16.1 45.5 %all-gather.2.cloned.1.call-done = bf16[16,512,128]{2,1,0:T(8,128)(2,1)} async-done(((bf16[2,512,128]{2,1,0:T(8,128)(2,1)}), bf16[16,512,128]{2,1,0:T(8,128)(2,1)}) %all-gather.2.cloned.1.call-update) | async-done | bytes 2097168 | tf_op jit(solution)/shard_map/all_gather | solution.py:87
  61.6 13.7 %while.38 = (s32[]{:T(128)}, f32[2,8,1,384]{3,2,1,0:T(1,128)S(1)}, bf16[2,8,512,128]{3,2,1,0:T(8,128)(2,1)}, bf16[1,256,512]{2,1,0:T(8,128)(2,1)S(1)}, s32[]{:T(128)}) while((s32[]{:T(128)}, f32[2,8,1,384]{3,2,1,0:T(1,128)S(1)}, bf16[2,8,512,128]{3,2,1,0:T(8,128)(2,1)}, bf16[1,256,512]{2,1,0:T(8,128)(2,1)S(1)}, s32[]{:T(128)}) %tuple.133), condition=%wide.region_2.3_spmd, body=%wide.region_0.2_spmd.sunk | while | flops 281021440 | bytes 108388928 | solution.py:108
  61.7 1.7 convolution_bitcast_fusion.3
  68.5 1.7 convolution_bitcast_fusion.3
  76.2 1.6 collective-permute-start.1
  77.8 1.4 collective-permute-start.2
  79.2 1.8 collective-permute-start.3
  81.0 1.6 collective-permute-start.4
  82.6 2.0 collective-permute-start.5
  84.6 2.4 %collective-permute-start.6 = (f32[1,2,1,384]{3,2,1,0:T(1,128)S(1)}, f32[1,2,1,384]{3,2,1,0:T(1,128)S(1)}, u32[]{:S(2)}, u32[]{:S(2)}) collective-permute-start(f32[1,2,1,384]{3,2,1,0:T(1,128)S(1)} %get-tuple-element.285), channel_id=1, source_target_pairs={{0,28},{4,24},{8,20},{12,16},{16,12},{20,8},{24,4},{28,0},{1,29},{... | collective-permute-start | bytes 9224 | tf_op jit(solution)/shard_map/ppermute | solution.py:117
  87.0 1.0 collective-permute-done.5
  88.0 2.9 %collective-permute-done.6 = f32[1,2,1,384]{3,2,1,0:T(1,128)S(1)} collective-permute-done((f32[1,2,1,384]{3,2,1,0:T(1,128)S(1)}, f32[1,2,1,384]{3,2,1,0:T(1,128)S(1)}, u32[]{:S(2)}, u32[]{:S(2)}) %collective-permute-start.6) | collective-permute-done | bytes 3104 | tf_op jit(solution)/shard_map/ppermute | solution.py:117
  91.6 39.2 %while.39 = (s32[]{:T(128)}, f32[1,2,2816]{2,1,0:T(2,128)S(1)}, s32[2,8]{1,0:T(2,128)S(1)}, f32[8,2,1,384]{3,2,1,0:T(1,128)S(1)}, s32[]{:T(128)}, /*index=5*/s32[]{:T(128)}, s32[]{:T(128)}, s32[]{}) while((s32[]{:T(128)}, f32[1,2,2816]{2,1,0:T(2,128)S(1)}, s32[2,8]{1,0:T(2,128)S(1)}, f32[8,2,1,384]{3,2,1,0:T(1,128)S(1)}, s32[]{:T(128)}, ...), condition=%wide.region_4.5_spmd, body=%wide.region_3.4_spmd.sunk | while | flops 777 | bytes 15573 | solution.py:127
  96.5 0.6 constant_dynamic-slice_fusion.10
  130.8 10.3 %psum.7 = f32[1,2,2816]{2,1,0:T(2,128)S(1)} all-reduce(f32[1,2,2816]{2,1,0:T(2,128)S(1)} %get-tuple-element.160), channel_id=1, replica_groups=mesh['blk'=8,'gy'=4] {'gy'}, use_global_device_ids=true, to_apply=%region_5.6 | all-reduce | flops 5632 | bytes 45056 | tf_op jit(solution)/shard_map/psum | solution.py:128
  141.1 10.9 %while.40 = (s32[]{:T(128)}, bf16[1,2816]{1,0:T(2,128)(2,1)S(1)}, s32[8,2]{0,1:T(2,128)S(1)}, bf16[8,1,384]{2,0,1:T(8,128)(2,1)S(1)}, s32[]{:T(128)}, /*index=5*/s32[]{:T(128)}) while((s32[]{:T(128)}, bf16[1,2816]{1,0:T(2,128)(2,1)S(1)}, s32[8,2]{0,1:T(2,128)S(1)}, bf16[8,1,384]{2,0,1:T(8,128)(2,1)S(1)}, s32[]{:T(128)}, /*index=5*/s32[]{:T(128)}) %tuple.125), condition=%wide.while_cond, body=%wide.while_body.sunk | while | flops 2 | bytes 3177 | solution.py:133
  141.7 0.7 dynamic-slice_bitcast_fusion.13
  143.1 0.7 dynamic-slice_bitcast_fusion.13
  144.5 0.7 dynamic-slice_bitcast_fusion.13
  145.8 0.7 dynamic-slice_bitcast_fusion.13
  147.2 0.7 dynamic-slice_bitcast_fusion.13
  148.6 0.7 dynamic-slice_bitcast_fusion.13
  149.9 0.7 dynamic-slice_bitcast_fusion.13
  151.3 0.7 dynamic-slice_bitcast_fusion.13
  152.1 10.2 %while.41 = (s32[]{:T(128)}, bf16[1,2816]{1,0:T(2,128)(2,1)S(1)}, s32[8,2]{0,1:T(2,128)S(1)}, bf16[8,1,384]{2,0,1:T(8,128)(2,1)S(1)}, s32[]{:T(128)}, /*index=5*/s32[]{:T(128)}) while((s32[]{:T(128)}, bf16[1,2816]{1,0:T(2,128)(2,1)S(1)}, s32[8,2]{0,1:T(2,128)S(1)}, bf16[8,1,384]{2,0,1:T(8,128)(2,1)S(1)}, s32[]{:T(128)}, /*index=5*/s32[]{:T(128)}) %tuple.122), condition=%wide.while_cond.1, body=%wide.while_body.1.sunk | while | flops 2 | bytes 3177 | solution.py:133
  162.9 3.6 %all-to-all-start = ((bf16[1,8,2,384]{3,2,0,1:T(2,128)(2,1)}), bf16[1,8,2,384]{3,2,0,1:T(2,128)(2,1)S(1)}, u32[]{:S(2)}, u32[]{:S(2)}) async-start(bf16[1,8,2,384]{3,2,0,1:T(2,128)(2,1)} %copy.33), calls=%async_computation | async-start | bytes 24576 | tf_op jit(solution)/shard_map/all_to_all | solution.py:143
  166.5 1.9 maximum_convert_fusion
  168.4 4.6 %all-to-all-done = bf16[1,8,2,384]{3,2,0,1:T(2,128)(2,1)S(1)} async-done(((bf16[1,8,2,384]{3,2,0,1:T(2,128)(2,1)}), bf16[1,8,2,384]{3,2,0,1:T(2,128)(2,1)S(1)}, u32[]{:S(2)}, u32[]{:S(2)}) %all-to-all-start) | async-done | bytes 12320 | tf_op jit(solution)/shard_map/all_to_all | solution.py:143
  173.0 29.1 %while.42 = (s32[]{:T(128)}, f32[1,256,512]{2,1,0:T(8,128)}, bf16[2,1,8,384]{3,2,0,1:T(8,128)(2,1)S(1)}, bf16[2,8,512,128]{3,2,1,0:T(8,128)(2,1)}, s32[]{:T(128)}, /*index=5*/s32[]{:T(128)}) while((s32[]{:T(128)}, f32[1,256,512]{2,1,0:T(8,128)}, bf16[2,1,8,384]{3,2,0,1:T(8,128)(2,1)S(1)}, bf16[2,8,512,128]{3,2,1,0:T(8,128)(2,1)}, ...), condition=%wide.region_7.8_spmd.clone, body=%wide.region_6.7_spmd.clone.sunk | while | flops 301471744 | bytes 67193432 | solution.py:158
  174.3 0.7 slice.374
  175.1 1.1 maximum_select_fusion.34
  176.3 0.7 slice.376
  177.1 0.7 maximum_select_fusion.35
  177.9 0.7 slice.378
  178.7 0.7 maximum_select_fusion.36
  179.5 0.7 slice.380
  180.3 0.7 maximum_select_fusion.37
  181.1 0.7 slice.382
  181.9 0.7 maximum_select_fusion.38
  182.7 0.7 slice.384
  183.5 0.7 maximum_select_fusion.39
  184.3 0.9 slice.385
  185.2 2.3 %fusion.42 = f32[1,256,512]{2,1,0:T(8,128)} fusion(bf16[2,8,512,128]{3,2,1,0:T(8,128)(2,1)S(1)} %copy-done, s32[]{:T(128)} %get-tuple-element.511, bf16[1,8,256,128]{3,2,1,0:T(8,128)(2,1)} %slice.385, bf16[1,8,256,256]{3,2,1,0:T(8,128)(2,1)S(1)} %slice.386, f32[1,256,512]{2,1,0:T(8,128)} %get-tuple-element.512, ...), kind=kOutput, calls=%fused_computation.43.clone.1 | convolution fusion | flops 270008320 | bytes 3670533 | tf_op jit(solution)/shard_map/while/body/eval_jaxpr/ytid,tzd->yiz/dot_general | solution.py:152
  188.8 0.7 slice.374
  189.6 1.1 maximum_select_fusion.34
  190.8 0.7 slice.376
  191.6 0.7 maximum_select_fusion.35
  192.4 0.7 slice.378
  193.2 0.7 maximum_select_fusion.36
  193.9 0.7 slice.380
  194.8 0.7 maximum_select_fusion.37
  195.5 0.7 slice.382
  196.4 0.7 maximum_select_fusion.38
  197.1 0.7 slice.384
  198.0 0.7 maximum_select_fusion.39
  198.8 0.9 slice.385
  199.7 2.5 %fusion.42 = f32[1,256,512]{2,1,0:T(8,128)} fusion(bf16[2,8,512,128]{3,2,1,0:T(8,128)(2,1)S(1)} %copy-done, s32[]{:T(128)} %get-tuple-element.511, bf16[1,8,256,128]{3,2,1,0:T(8,128)(2,1)} %slice.385, bf16[1,8,256,256]{3,2,1,0:T(8,128)(2,1)S(1)} %slice.386, f32[1,256,512]{2,1,0:T(8,128)} %get-tuple-element.512, ...), kind=kOutput, calls=%fused_computation.43.clone.1 | convolution fusion | flops 270008320 | bytes 3670533 | tf_op jit(solution)/shard_map/while/body/eval_jaxpr/ytid,tzd->yiz/dot_general | solution.py:152
  202.2 2.8 %fusion.19 = f32[1,256,512]{2,1,0:T(8,128)} fusion(f32[1,256,514]{2,1,0:T(8,128)} %maximum_convert_fusion, f32[1,256,512]{2,1,0:T(8,128)} %param.12, f32[1,256,512]{2,1,0:T(8,128)} %get-tuple-element.161, f32[256,512]{1,0:T(8,128)} %param.15), kind=kLoop, calls=%fused_computation.66 | loop fusion | flops 917504 | bytes 3145728 | tf_op jit(solution)/shard_map/add | solution.py:161
  (258 shorter events, 40.7 us)
Async XLA Ops:
  6.5 55.1 %all-gather.2.cloned.1.call-start = ((), (), s32[]{:S(2)}) async-start(), calls=%async_computation.1 | async-start | bytes 2359296 | tf_op jit(solution)/shard_map/all_gather | solution.py:87
  9.0 157.4 %collective-permute-start.7 = (bf16[1,256,1]{2,1,0:T(8,128)(2,1)}, bf16[1,256,1]{2,1,0:T(8,128)(2,1)}, u32[]{:S(2)}, u32[]{:S(2)}) collective-permute-start(bf16[1,256,1]{2,1,0:T(8,128)(2,1)} %get-tuple-element.283), channel_id=1, source_target_pairs={{0,1},{1,2},{2,3},{4,5},{5,6},{6,7},{8,9},{9,10},{10,11},{12,13},{... | collective-permute-start | bytes 1544 | tf_op jit(solution)/shard_map/ppermute | solution.py:36
  12.0 154.5 %collective-permute-start.8 = (bf16[1,256,1]{2,1,0:T(8,128)(2,1)}, bf16[1,256,1]{2,1,0:T(8,128)(2,1)}, u32[]{:S(2)}, u32[]{:S(2)}) collective-permute-start(bf16[1,256,1]{2,1,0:T(8,128)(2,1)} %get-tuple-element.284), channel_id=1, source_target_pairs={{1,0},{2,1},{3,2},{5,4},{6,5},{7,6},{9,8},{10,9},{11,10},{13,12},{... | collective-permute-start | bytes 1544 | tf_op jit(solution)/shard_map/ppermute | solution.py:38
  14.7 0.6 copy-start.1
  61.6 14.4 %copy-start.7 = (s32[8]{0:T(128)S(1)}, s32[8]{0:T(128)}, u32[]{:S(2)}) copy-start(s32[8]{0:T(128)} %fusion.22) | copy-start | bytes 100
  61.6 14.5 %copy-start.2 = (s32[2,8]{0,1:T(8,128)S(1)}, s32[2,8]{0,1:T(8,128)}, u32[]{:S(2)}) copy-start(s32[2,8]{0,1:T(8,128)} %copy-done.1) | copy-start | bytes 196
  61.6 14.5 %copy-start.6 = (s32[8,1]{0,1:T(1,128)S(1)}, s32[8,1]{0,1:T(1,128)}, u32[]{:S(2)}) copy-start(s32[8,1]{0,1:T(1,128)} %get-tuple-element.296) | copy-start | bytes 100
  61.6 14.6 %copy-start.5 = (s32[8,1]{0,1:T(1,128)S(1)}, s32[8,1]{0,1:T(1,128)}, u32[]{:S(2)}) copy-start(s32[8,1]{0,1:T(1,128)} %get-tuple-element.295) | copy-start | bytes 100
  61.6 79.4 %copy-start.3 = (f32[2,2816]{1,0:T(2,128)S(1)}, f32[2,2816]{1,0:T(2,128)}, u32[]{:S(2)}) copy-start(f32[2,2816]{1,0:T(2,128)} %param.14) | copy-start | bytes 67588
  61.6 79.4 %copy-start.4 = (f32[1,2,2816]{2,1,0:T(2,128)S(1)}, f32[1,2,2816]{2,1,0:T(2,128)}, u32[]{:S(2)}) copy-start(f32[1,2,2816]{2,1,0:T(2,128)} %param.13) | copy-start | bytes 67588
  75.4 3.8 %collective-permute-start = (f32[1,2,1,384]{3,2,1,0:T(1,128)S(1)}, f32[1,2,1,384]{3,2,1,0:T(1,128)S(1)}, u32[]{:S(2)}, u32[]{:S(2)}) collective-permute-start(f32[1,2,1,384]{3,2,1,0:T(1,128)S(1)} %get-tuple-element.291), channel_id=1, source_target_pairs={{0,4},{4,0},{8,12},{12,8},{16,20},{20,16},{24,28},{28,24},{1,5},{5... | collective-permute-start | bytes 9224 | tf_op jit(solution)/shard_map/ppermute | solution.py:117
  76.2 4.8 %collective-permute-start.1 = (f32[1,2,1,384]{3,2,1,0:T(1,128)S(1)}, f32[1,2,1,384]{3,2,1,0:T(1,128)S(1)}, u32[]{:S(2)}, u32[]{:S(2)}) collective-permute-start(f32[1,2,1,384]{3,2,1,0:T(1,128)S(1)} %get-tuple-element.290), channel_id=1, source_target_pairs={{0,8},{4,12},{8,0},{12,4},{16,24},{20,28},{24,16},{28,20},{1,9},{5... | collective-permute-start | bytes 9224 | tf_op jit(solution)/shard_map/ppermute | solution.py:117
  77.8 4.9 %collective-permute-start.2 = (f32[1,2,1,384]{3,2,1,0:T(1,128)S(1)}, f32[1,2,1,384]{3,2,1,0:T(1,128)S(1)}, u32[]{:S(2)}, u32[]{:S(2)}) collective-permute-start(f32[1,2,1,384]{3,2,1,0:T(1,128)S(1)} %get-tuple-element.289), channel_id=1, source_target_pairs={{0,12},{4,8},{8,4},{12,0},{16,28},{20,24},{24,20},{28,16},{1,13},{... | collective-permute-start | bytes 9224 | tf_op jit(solution)/shard_map/ppermute | solution.py:117
  79.2 5.4 %collective-permute-start.3 = (f32[1,2,1,384]{3,2,1,0:T(1,128)S(1)}, f32[1,2,1,384]{3,2,1,0:T(1,128)S(1)}, u32[]{:S(2)}, u32[]{:S(2)}) collective-permute-start(f32[1,2,1,384]{3,2,1,0:T(1,128)S(1)} %get-tuple-element.288), channel_id=1, source_target_pairs={{0,16},{4,20},{8,24},{12,28},{16,0},{20,4},{24,8},{28,12},{1,17},{... | collective-permute-start | bytes 9224 | tf_op jit(solution)/shard_map/ppermute | solution.py:117
  81.0 6.0 %collective-permute-start.4 = (f32[1,2,1,384]{3,2,1,0:T(1,128)S(1)}, f32[1,2,1,384]{3,2,1,0:T(1,128)S(1)}, u32[]{:S(2)}, u32[]{:S(2)}) collective-permute-start(f32[1,2,1,384]{3,2,1,0:T(1,128)S(1)} %get-tuple-element.287), channel_id=1, source_target_pairs={{0,20},{4,16},{8,28},{12,24},{16,4},{20,0},{24,12},{28,8},{1,21},{... | collective-permute-start | bytes 9224 | tf_op jit(solution)/shard_map/ppermute | solution.py:117
  82.6 5.4 %collective-permute-start.5 = (f32[1,2,1,384]{3,2,1,0:T(1,128)S(1)}, f32[1,2,1,384]{3,2,1,0:T(1,128)S(1)}, u32[]{:S(2)}, u32[]{:S(2)}) collective-permute-start(f32[1,2,1,384]{3,2,1,0:T(1,128)S(1)} %get-tuple-element.286), channel_id=1, source_target_pairs={{0,24},{4,28},{8,16},{12,20},{16,8},{20,12},{24,0},{28,4},{1,25},{... | collective-permute-start | bytes 9224 | tf_op jit(solution)/shard_map/ppermute | solution.py:117
  84.6 6.3 %collective-permute-start.6 = (f32[1,2,1,384]{3,2,1,0:T(1,128)S(1)}, f32[1,2,1,384]{3,2,1,0:T(1,128)S(1)}, u32[]{:S(2)}, u32[]{:S(2)}) collective-permute-start(f32[1,2,1,384]{3,2,1,0:T(1,128)S(1)} %get-tuple-element.285), channel_id=1, source_target_pairs={{0,28},{4,24},{8,20},{12,16},{16,12},{20,8},{24,4},{28,0},{1,29},{... | collective-permute-start | bytes 9224 | tf_op jit(solution)/shard_map/ppermute | solution.py:117
  162.9 10.2 %all-to-all-start = ((bf16[1,8,2,384]{3,2,0,1:T(2,128)(2,1)}), bf16[1,8,2,384]{3,2,0,1:T(2,128)(2,1)S(1)}, u32[]{:S(2)}, u32[]{:S(2)}) async-start(bf16[1,8,2,384]{3,2,0,1:T(2,128)(2,1)} %copy.33), calls=%async_computation | async-start | bytes 24576 | tf_op jit(solution)/shard_map/all_to_all | solution.py:143
  183.5 1.7 copy-start
  198.0 1.7 copy-start
Sparse Core Ops, SparseCore 0:
  9.5 52.0 all-gather.1
